TPU v7x, 32 devices: a whole 2x2x4 slice. The times are simulated.
32 devices in a mesh: groups: 2 (over x), genome: 16 (over z, y, core).
Axes of the slice: x: 2, y: 2, z: 4, core: 2. Of those that a mesh axis runs over, the one named last changes fastest.
Arguments:
- factor: bfloat16 [96, 2048, 256], P(('groups', 'genome')), parts along dimension 0, may hold values from -0.5 to 0.5
- normals: bfloat16 [96, 256, 1024], P(('groups', 'genome')), parts along dimension 0, may hold values from -6 to 6
- block_len: int32 [96], P(('groups', 'genome')), parts along dimension 0, may hold values from 256 to 2048, as said below
- block_rank: int32 [96], P(('groups', 'genome')), parts along dimension 0, may hold values from 32 to 256, as said below
- gene_span: int32 [2048, 2], P(('groups', 'genome')), parts along dimension 0, may hold values from 0 to 98304, as said below
- gene_pathways: int32 [2048, 4], P('groups'), parts along dimension 0, may hold values from 0 to 4095, as said below
Outputs:
- pathway_score: float32 [8192, 1024], P(('groups', 'genome')), parts along dimension 0
There are 2 independent parts, one for each index of `groups`. A program takes and returns all parts, laid end to end along the dimension named above; each array names one. Nothing has to cross between parts.
Inputs may be any that keep to these rules, and one draw needn't show every extreme that they name: `block_len`: some block of every draw holds all 2048 slots. `block_rank`: some block of every draw keeps all 256 columns. `gene_span`: genes of rows j * 64 to (j + 1) * 64 - 1 start at a valid slot within slots j * 6144 to (j + 1) * 6144 - 1 and end no later than (j + 1) * 6144 + 2048, never past 98304; the end exceeds the start; some gene of every draw ends exactly 2048 slots past the range of its start. Each gene names 4 different pathways, and every pathway is named by some gene. With q = g * 4 + m, the pathway gene_pathways[g, m] lies in rows r * 256 to (r + 1) * 256 - 1 with r = q % 16, so the genes of one index of genome name at most 16 pathways of one such range, and exactly 16 for some range.
All inputs are finite; a program needn't handle non-finite values.
Results may differ from a plain program's by a relative error of at most 0.0021.
Values may be sent and summed in bfloat16 or wider, within the bound.
A program may use at most 128 MiB of HBM per device.

v0:
```python
import jax
import jax.numpy as jnp
from jax import lax
from jax.sharding import PartitionSpec as P

PATHWAYS = 4096


def shifted(block, axis, distance):
    devices = range(lax.axis_size(axis))
    route = [(i - distance, i) for i in devices if i - distance in devices]
    return lax.ppermute(block, axis, route)


def covered(positions, spans):
    lower = spans[:, 0][:, None]
    upper = spans[:, 1][:, None]
    return ((positions[None, :] >= lower) & (positions[None, :] < upper)).astype(jnp.float32)


def local(factor, normals, block_len, block_rank, gene_span, gene_pathways):
    block_count, capacity, rank_cap = factor.shape
    sim_count = normals.shape[2]
    local_vars = block_count * capacity
    gene_count = gene_span.shape[0]
    member_count = gene_pathways.shape[1]
    device = lax.axis_index("genome")
    devices_n = lax.axis_size("genome")
    offset = device * local_vars
    kept = jnp.arange(rank_cap, dtype=jnp.int32)[None, :, None] < block_rank[:, None, None]
    trimmed = jnp.where(kept, normals, jnp.zeros_like(normals))
    row_ids = jnp.arange(capacity, dtype=jnp.int32)
    totals = jnp.zeros((gene_count, sim_count), jnp.float32)
    leading = None
    for block in range(block_count):
        coloured = jnp.dot(factor[block], trimmed[block], preferred_element_type=jnp.float32)
        usable = row_ids < block_len[block]
        squares = jnp.where(usable[:, None], coloured * coloured, 0.0)
        positions = offset + block * capacity + row_ids
        totals = totals + jnp.dot(
            covered(positions, gene_span), squares, precision=lax.Precision.HIGHEST
        )
        if block == 0:
            leading = squares
    following = shifted(leading, "genome", -1)
    beyond = offset + local_vars + row_ids
    totals = totals + jnp.dot(
        covered(beyond, gene_span), following, precision=lax.Precision.HIGHEST
    )
    gene_stat = (totals / capacity).astype(jnp.bfloat16)
    path_rows = PATHWAYS // devices_n
    own_ids = device * path_rows + jnp.arange(path_rows, dtype=jnp.int32)
    pair_count = gene_count * member_count
    slot_count = (pair_count + devices_n - 1) // devices_n
    owners = jnp.arange(devices_n, dtype=jnp.int32)[:, None]
    slot_ids = jnp.arange(slot_count, dtype=jnp.int32)[None, :]
    own_shift = device * pair_count % devices_n
    local_pair = (owners - own_shift) % devices_n + slot_ids * devices_n
    valid_send = local_pair < pair_count
    gene_rows = jnp.where(valid_send, local_pair // member_count, 0)
    packed = jnp.where(valid_send[:, :, None], gene_stat[gene_rows], jnp.zeros((), jnp.bfloat16))
    received = lax.all_to_all(packed, "genome", split_axis=0, concat_axis=0, tiled=True)
    sources = jnp.arange(devices_n, dtype=jnp.int32)[:, None]
    source_shift = sources * pair_count % devices_n
    their_pair = (device - source_shift) % devices_n + slot_ids * devices_n
    valid_take = their_pair < pair_count
    global_pair = jnp.where(valid_take, sources * pair_count + their_pair, 0)
    local_path = gene_pathways.reshape(-1)[global_pair] - device * path_rows
    local_path = jnp.where(valid_take, local_path, -1).reshape(-1)
    member = (local_path[None, :] == jnp.arange(path_rows, dtype=jnp.int32)[:, None]).astype(
        jnp.bfloat16
    )
    summed = jnp.dot(
        member,
        received.reshape(devices_n * slot_count, sim_count),
        preferred_element_type=jnp.float32,
    )
    path_count = jnp.sum(
        (gene_pathways.reshape(-1)[None, :] == own_ids[:, None]).astype(jnp.float32), axis=1
    )
    return summed / path_count[:, None]


def solution(mesh):
    in_specs = (
        P(("groups", "genome"), None, None),
        P(("groups", "genome"), None, None),
        P(("groups", "genome")),
        P(("groups", "genome")),
        P(("groups", "genome"), None),
        P("groups", None),
    )
    out_specs = P(("groups", "genome"), None)
    return jax.shard_map(local, mesh=mesh, in_specs=in_specs, out_specs=out_specs, check_vma=False)
```

profile of v0, /device:TPU:0, one launch (start us, length us, event | category | flops | bytes accessed | tf_op | source)
XLA Modules:
  0.0 140.1 jit_solution(4006993111875055616)
XLA Ops:
  0.0 0.7 iota_compare_fusion.5
  0.7 1.4 fusion.67
  2.1 0.7 iota_compare_fusion.4
  2.7 1.6 %broadcast_select_fusion = bf16[3,256,1024]{2,1,0:T(8,128)(2,1)S(1)} fusion(bf16[3,256,1024]{2,1,0:T(8,128)(2,1)} %param.7, pred[3,256]{1,0:T(4,128)(4,1)S(1)} %iota_compare_fusion.5), kind=kLoop, calls=%fused_computation.18 | loop fusion | flops 786432 | bytes 3146496 | tf_op jit(solution)/shard_map/jit(_where)/select_n | solution.py:31
  4.3 2.5 %fusion.22 = f32[1024,2048]{1,0:T(8,128)S(1)} fusion(bf16[3,2048,256]{2,1,0:T(8,128)(2,1)} %param.6, bf16[3,256,1024]{2,1,0:T(8,128)(2,1)S(1)} %broadcast_select_fusion), kind=kOutput, calls=%fused_computation.29 | convolution fusion | flops 1073741824 | bytes 9961472 | tf_op jit(solution)/shard_map/dot_general | solution.py:36
  6.9 0.0 copy-start
  6.9 0.0 copy-start.2
  6.9 4.7 %fusion.6 = f32[2048,1024]{0,1:T(8,128)} fusion(f32[1024,2048]{1,0:T(8,128)S(1)} %fusion.22, pred[2048]{0:T(1024)(128)(4,1)S(1)} %iota_compare_fusion.4), kind=kLoop, calls=%fused_computation.9 | loop fusion | flops 4194304 | bytes 16779264 | tf_op jit(solution)/shard_map/jit(_where)/select_n | solution.py:38
  11.6 1.0 copy-done
  12.6 1.5 %collective-permute-start = (f32[2048,1024]{0,1:T(8,128)}, f32[2048,1024]{0,1:T(8,128)}, u32[]{:S(2)}, u32[]{:S(2)}) collective-permute-start(f32[2048,1024]{0,1:T(8,128)} %fusion.6), channel_id=1, source_target_pairs={{1,0},{2,1},{3,2},{4,3},{5,4},{6,5},{7,6},{8,7},{9,8},{10,9},{11,1... | collective-permute-start | bytes 25165832 | tf_op jit(solution)/shard_map/ppermute | solution.py:12
  14.1 0.1 compare_select_fusion.1
  14.2 0.1 reshape.384
  14.3 0.6 iota_compare_fusion.2
  14.9 0.6 iota_compare_fusion.3
  15.5 0.0 copy-done.2
  15.5 0.1 add_compare_fusion.3
  15.6 2.5 %fusion.18 = f32[1024,2048]{1,0:T(8,128)S(1)} fusion(bf16[3,2048,256]{2,1,0:T(8,128)(2,1)} %param.6, bf16[3,256,1024]{2,1,0:T(8,128)(2,1)S(1)} %broadcast_select_fusion), kind=kOutput, calls=%fused_computation.25 | convolution fusion | flops 1073741824 | bytes 9961472 | tf_op jit(solution)/shard_map/dot_general | solution.py:36
  18.2 2.5 %fusion.20 = f32[1024,2048]{1,0:T(8,128)S(1)} fusion(bf16[3,2048,256]{2,1,0:T(8,128)(2,1)} %param.6, bf16[3,256,1024]{2,1,0:T(8,128)(2,1)S(1)} %broadcast_select_fusion), kind=kOutput, calls=%fused_computation.27 | convolution fusion | flops 1073741824 | bytes 9961472 | tf_op jit(solution)/shard_map/dot_general | solution.py:36
  20.7 0.0 slice-start
  20.7 5.0 %fusion = f32[64,1024]{1,0:T(8,128)S(1)} fusion(f32[1024,2048]{1,0:T(8,128)S(1)} %fusion.18, pred[2048]{0:T(1024)(128)(4,1)S(1)} %iota_compare_fusion.2, s32[2048]{0:T(1024)S(1)} %iota_add_fusion.1, s32[64]{0:T(128)S(1)} %get-tuple-element.6, s32[64]{0:T(128)S(1)} %get-tuple-element.5), kind=kOutput, calls=%fused_computation.2 | convolution fusion | flops 1615200256 | bytes 8661504 | tf_op jit(solution)/shard_map/dot_general | solution.py:40
  25.7 0.0 slice-start.1
  25.7 5.0 %fusion.3 = f32[64,1024]{1,0:T(8,128)S(1)} fusion(f32[1024,2048]{1,0:T(8,128)S(1)} %fusion.20, pred[2048]{0:T(1024)(128)(4,1)S(1)} %iota_compare_fusion.3, s32[2048]{0:T(1024)S(1)} %iota_add_fusion.2, s32[64]{0:T(128)S(1)} %get-tuple-element.6, s32[64]{0:T(128)S(1)} %get-tuple-element.5), kind=kOutput, calls=%fused_computation.5 | convolution fusion | flops 1615200256 | bytes 8661504 | tf_op jit(solution)/shard_map/dot_general | solution.py:40
  30.7 0.0 slice-done
  30.7 0.0 slice-done.1
  30.7 5.2 %fusion.16 = f32[64,1024]{1,0:T(8,128)S(1)} fusion(f32[64,1024]{1,0:T(8,128)S(1)} %fusion, f32[64,1024]{1,0:T(8,128)S(1)} %fusion.3, f32[1024,2048]{1,0:T(8,128)S(1)} %bitcast.36, pred[2048]{0:T(1024)(128)(4,1)S(1)} %iota_compare_fusion.4, s32[2048]{0:T(1024)S(1)} %iota_add_fusion.3, s32[64]{0:T(128)S(1)} %get-tuple-element.6, s32[64]{0:T(128)S(1)} %get-tuple-element.5), kind=kOutput, calls=%fused_computation.23 | convolution fusion | flops 1615331328 | bytes 9185792 | tf_op jit(solution)/shard_map/dot_general | solution.py:40
  35.9 0.0 copy-start.1
  35.9 0.0 collective-permute-done
  35.9 7.9 %fusion.17 = bf16[64,1024]{1,0:T(8,128)(2,1)S(1)} fusion(f32[64,1024]{1,0:T(8,128)S(1)} %fusion.16, f32[2048,1024]{0,1:T(8,128)} %collective-permute-done, s32[2048]{0:T(1024)S(1)} %iota_add_fusion, s32[64]{0:T(128)S(1)} %get-tuple-element.6, s32[64]{0:T(128)S(1)} %get-tuple-element.5), kind=kOutput, calls=%fused_computation.24 | convolution fusion | flops 1611202560 | bytes 8790528 | tf_op jit(solution)/shard_map/dot_general | solution.py:47
  43.8 1.2 gather_fusion.1
  45.0 0.9 broadcast_select_fusion.1
  45.9 78.5 %all-to-all-start = ((bf16[16,16,1024]{2,1,0:T(8,128)(2,1)}), bf16[16,16,1024]{2,1,0:T(8,128)(2,1)S(1)}, u32[]{:S(2)}, u32[]{:S(2)}) async-start(bf16[16,16,1024]{2,1,0:T(8,128)(2,1)} %broadcast_select_fusion.1), calls=%async_computation | async-start | bytes 1048576 | tf_op jit(solution)/shard_map/all_to_all | solution.py:62
  124.4 0.0 copy-done.1
  124.4 0.2 copy.8
  124.6 0.3 reshape.372
  124.9 0.1 reshape.376
  125.0 1.7 %gather_fusion = s32[256]{0:T(256)S(1)} fusion(s32[4096]{0:T(1024)S(1)} %reshape.372, s32[1024]{0:T(1024)S(1)} %pad_clamp_fusion.1), kind=kCustom, calls=%fused_computation | custom fusion | bytes 3072 | tf_op jit(solution)/shard_map/gather | solution.py:68
  126.7 0.1 reshape.393
  126.8 0.1 fusion.59
  126.9 0.1 select_n.127
  127.0 0.6 convert_reduce_fusion
  127.5 11.3 %all-to-all-done = bf16[16,16,1024]{2,1,0:T(8,128)(2,1)S(1)} async-done(((bf16[16,16,1024]{2,1,0:T(8,128)(2,1)}), bf16[16,16,1024]{2,1,0:T(8,128)(2,1)S(1)}, u32[]{:S(2)}, u32[]{:S(2)}) %all-to-all-start) | async-done | bytes 524320 | tf_op jit(solution)/shard_map/all_to_all | solution.py:62
  138.8 1.3 convolution_divide_fusion
  (12 shorter events, 0.1 us)
Async XLA Ops:
  6.9 5.7 %copy-start = (f32[1024,2048]{1,0:T(8,128)}, f32[1024,2048]{1,0:T(8,128)S(1)}, u32[]{:S(2)}) copy-start(f32[1024,2048]{1,0:T(8,128)S(1)} %fusion.22) | copy-start | bytes 25165828
  6.9 8.6 %copy-start.2 = (s32[64,2]{0,1:T(2,128)S(1)}, s32[64,2]{0,1:T(2,128)}, u32[]{:S(2)}) copy-start(s32[64,2]{0,1:T(2,128)} %param.10) | copy-start | bytes 1540
  12.6 23.3 %collective-permute-start = (f32[2048,1024]{0,1:T(8,128)}, f32[2048,1024]{0,1:T(8,128)}, u32[]{:S(2)}, u32[]{:S(2)}) collective-permute-start(f32[2048,1024]{0,1:T(8,128)} %fusion.6), channel_id=1, source_target_pairs={{1,0},{2,1},{3,2},{4,3},{5,4},{6,5},{7,6},{8,7},{9,8},{10,9},{11,1... | collective-permute-start | bytes 25165832 | tf_op jit(solution)/shard_map/ppermute | solution.py:12
  20.7 10.0 %slice-start = ((s8[8388608]{0:T(1024)(128)(4,1)}), s8[4194304]{0:T(1024)(128)(4,1)S(1)}, s32[]{:S(2)}) async-start(s8[8388608]{0:T(1024)(128)(4,1)} %bitcast.35), calls=%async_computation.1 | async-start | bytes 8388608
  25.7 5.0 %slice-start.1 = ((s8[8388608]{0:T(1024)(128)(4,1)}), s8[4194304]{0:T(1024)(128)(4,1)S(1)}, s32[]{:S(2)}) async-start(s8[8388608]{0:T(1024)(128)(4,1)} %bitcast.35), calls=%async_computation.2 | async-start | bytes 8388608
  35.9 88.5 %copy-start.1 = (s32[1024,4]{0,1:T(4,128)S(1)}, s32[1024,4]{0,1:T(4,128)}, u32[]{:S(2)}) copy-start(s32[1024,4]{0,1:T(4,128)} %param.11) | copy-start | bytes 49156
  45.9 93.0 %all-to-all-start = ((bf16[16,16,1024]{2,1,0:T(8,128)(2,1)}), bf16[16,16,1024]{2,1,0:T(8,128)(2,1)S(1)}, u32[]{:S(2)}, u32[]{:S(2)}) async-start(bf16[16,16,1024]{2,1,0:T(8,128)(2,1)} %broadcast_select_fusion.1), calls=%async_computation | async-start | bytes 1048576 | tf_op jit(solution)/shard_map/all_to_all | solution.py:62
where the time goes:
time: 141 us; the launch traced here: 140 us
  starting transfers between devices  80 us (57%)
  matrix products  31.9 us (23%)
  waiting for transfers between devices  11.3 us (8%)
  other arithmetic  10.6 us (8%)
  local copies, waits for them, and re-layouts  6.12 us (4%)
    all_to_all x1, starting transfers between devices, local(): lax.all_to_all(packed, 'genome', split_axis=0, concat_axis=0, tiled=True)  78.5 us
    dot_general x3, matrix products, local(): jnp.dot(covered(positions, gene_span), squares, precision=lax.Precision.H...  15.1 us
    all_to_all x1, waiting for transfers between devices, local(): lax.all_to_all(packed, 'genome', split_axis=0, concat_axis=0, tiled=True)  11.3 us
    dot_general x1, matrix products, local(): jnp.dot(covered(beyond, gene_span), following, precision=lax.Precision.HI...  7.89 us
    dot_general x3, matrix products, local(): jnp.dot(factor[block], trimmed[block], preferred_element_type=jnp.float32)  7.61 us
    select_n x1, other arithmetic, local(): squares = jnp.where(usable[:, None], coloured * coloured, 0.0)  4.67 us
  transfers between devices with their start and end apart: 2, of which 1 were waited for; matrix products, arithmetic and copies ran while one was open for 18% of the time, Pallas kernels for 0%

commit v1 on v0

v1 whole, which is shorter than its diff:
```python
import functools

import jax
import jax.numpy as jnp
from jax import lax
from jax.experimental import pallas as pl
from jax.experimental.pallas import tpu as pltpu
from jax.sharding import PartitionSpec as P

PATHWAYS = 4096
TILE = 512
QUAD = 4


def kernel(
    n, genes, rows,
    len_ref, rank_ref, span_ref, paths_ref, factor_ref, normals_ref,
    out_ref,
    fac, nrm, sums, partial, halo, own_span, pred_span, stat, gathered, member, count,
    fac_sem, nrm_sem, span_send, span_recv, halo_send, halo_recv,
    col_send, col_recv, quad_send, quad_recv,
):
    quads = n // QUAD
    blocks, capacity, rank_cap = factor_ref.shape
    sims = normals_ref.shape[2]
    local_vars = blocks * capacity
    padded = quads * rows
    me = lax.axis_index("genome")
    right, left = lax.rem(me + 1, n), lax.rem(me + n - 1, n)
    quad, lane = me // QUAD, lax.rem(me, QUAD)
    column = [lax.rem(quad + d, quads) * QUAD + lane for d in range(1, quads)]
    peers = [quad * QUAD + lax.rem(lane + e, QUAD) for e in range(1, QUAD)]

    order = [1, 0, 2] if blocks == 3 else list(range(1, blocks)) + [0]
    fac_copies, nrm_copies = {}, {}
    for b in order:
        nrm_copies[b] = pltpu.make_async_copy(normals_ref.at[b], nrm.at[b], nrm_sem.at[b])
        fac_copies[b] = pltpu.make_async_copy(factor_ref.at[b], fac.at[b], fac_sem.at[b])
        nrm_copies[b].start()
        fac_copies[b].start()

    barrier = pltpu.get_barrier_semaphore()
    greeted = [left, right] + column + peers
    for device in greeted:
        pl.semaphore_signal(barrier, inc=1, device_id={"genome": device})

    share = genes // quads
    row = lax.broadcasted_iota(jnp.int32, (padded, genes), 0)
    col = lax.broadcasted_iota(jnp.int32, (padded, genes), 1)
    within = row % rows
    placed = (row // rows + quads * within == col) & (within < share)

    def columns_of(spans):
        lower = jnp.sum(jnp.where(placed, spans[0:1, :genes], 0.0), axis=1, keepdims=True)
        upper = jnp.sum(jnp.where(placed, spans[1:2, :genes], 0.0), axis=1, keepdims=True)
        return lower.astype(jnp.int32), upper.astype(jnp.int32)

    own_span[...] = jnp.zeros_like(own_span)
    own_span[0:2, 0:genes] = span_ref[...].astype(jnp.float32)
    lower, upper = columns_of(own_span[...])
    sums[...] = jnp.zeros_like(sums)

    def trim(b):
        nrm_copies[b].wait()
        ids = lax.broadcasted_iota(jnp.int32, (rank_cap, sims), 0)
        values = nrm[b].astype(jnp.float32)
        nrm[b] = jnp.where(ids < rank_ref[b], values, 0.0).astype(jnp.bfloat16)

    def add_tile(b, step, spans):
        first = step * TILE
        coloured = jnp.dot(
            fac[b, pl.ds(first, TILE), :], nrm[b], preferred_element_type=jnp.float32
        )
        squares = (coloured * coloured).astype(jnp.bfloat16)
        start = me * local_vars + b * capacity
        limit = start + len_ref[b]
        for into, low, high in spans:
            place = start + first + lax.broadcasted_iota(jnp.int32, (padded, TILE), 1)
            inside = (place >= low) & (place < jnp.minimum(high, limit))
            into[...] += jnp.dot(
                inside.astype(jnp.float32).astype(jnp.bfloat16),
                squares,
                preferred_element_type=jnp.float32,
            )

    def add_block(b, spans, begin=0, end=None):
        for step in range(begin, capacity // TILE if end is None else end):
            add_tile(b, step, spans)

    own = [(sums, lower, upper)]
    b = order[0]
    trim(b)
    fac_copies[b].wait()
    half = capacity // TILE // 2
    add_block(b, own, 0, half)
    pl.semaphore_wait(barrier, len(greeted))
    span_copy = pltpu.make_async_remote_copy(
        own_span, pred_span, span_send, span_recv, device_id={"genome": right}
    )
    span_copy.start()
    add_block(b, own, half)
    for b in order[1:]:
        trim(b)
        fac_copies[b].wait()
        if b == 0:
            span_copy.wait()
            partial[...] = jnp.zeros_like(partial)
            pred_lower, pred_upper = columns_of(pred_span[...])
            add_block(b, own + [(partial, pred_lower, pred_upper)])
            halo_copy = pltpu.make_async_remote_copy(
                partial, halo, halo_send, halo_recv, device_id={"genome": left}
            )

            @pl.when(me > 0)
            def _():
                halo_copy.start()
        else:
            add_block(b, own)

    path_rows, total_genes = out_ref.shape[0], paths_ref.shape[1]
    slots = n * rows
    named = paths_ref[pl.ds(lane, 1), :] - me * path_rows
    ids = lax.broadcasted_iota(jnp.int32, (path_rows, total_genes), 0)
    names = (named == ids).astype(jnp.float32).astype(jnp.bfloat16)
    gene = lax.broadcasted_iota(jnp.int32, (total_genes, slots), 0)
    slot = lax.broadcasted_iota(jnp.int32, (total_genes, slots), 1)
    takes = (gene // genes) * rows + (gene % genes) // quads == slot
    chosen = jnp.dot(
        names, takes.astype(jnp.float32).astype(jnp.bfloat16), preferred_element_type=jnp.float32
    )
    count[...] = jnp.sum(chosen, axis=1, keepdims=True)
    member[...] = chosen.astype(jnp.bfloat16)

    scale = 1.0 / capacity

    @pl.when(me < n - 1)
    def _():
        halo_copy.wait_recv()
        stat[...] = ((sums[...] + halo[...]) * scale).astype(jnp.bfloat16)

    @pl.when(me == n - 1)
    def _():
        stat[...] = (sums[...] * scale).astype(jnp.bfloat16)

    @pl.when(me > 0)
    def _():
        halo_copy.wait_send()

    sent = []
    for d in range(1, quads):
        target = lax.rem(quad + d, quads)
        copy = pltpu.make_async_remote_copy(
            stat.at[pl.ds(pl.multiple_of(target * rows, rows), rows)],
            gathered.at[pl.ds(pl.multiple_of(me * rows, rows), rows)],
            col_send.at[d], col_recv.at[d],
            device_id={"genome": target * QUAD + lane},
        )
        copy.start()
        sent.append(copy)
    gathered[pl.ds(pl.multiple_of(me * rows, rows), rows), :] = stat[
        pl.ds(pl.multiple_of(quad * rows, rows), rows), :
    ]

    def forward(d):
        source = lax.rem(quad + quads - d, quads) * QUAD + lane
        block = gathered.at[pl.ds(pl.multiple_of(source * rows, rows), rows)]
        for e in range(1, QUAD):
            copy = pltpu.make_async_remote_copy(
                block, block, quad_send.at[d, e], quad_recv.at[d, e],
                device_id={"genome": peers[e - 1]},
            )
            copy.start()
            sent.append(copy)

    forward(0)
    for d in range(1, quads):
        sent[d - 1].wait_recv()
        forward(d)
    for copy in sent[quads - 1:]:
        copy.wait_recv()
    summed = jnp.dot(member[...], gathered[...], preferred_element_type=jnp.float32)
    out_ref[...] = summed / count[...]
    for copy in sent:
        copy.wait_send()


def local(factor, normals, block_len, block_rank, gene_span, gene_pathways):
    blocks, capacity, rank_cap = factor.shape
    sims = normals.shape[2]
    genes = gene_span.shape[0]
    n = lax.axis_size("genome")
    quads = n // QUAD
    rows = max(16, genes // quads)
    padded = quads * rows
    path_rows = PATHWAYS // n
    vmem = pl.BlockSpec(memory_space=pltpu.VMEM)
    smem = pl.BlockSpec(memory_space=pltpu.SMEM)
    hbm = pl.BlockSpec(memory_space=pl.ANY)
    dma = pltpu.SemaphoreType.DMA
    return pl.pallas_call(
        functools.partial(kernel, n, genes, rows),
        out_shape=jax.ShapeDtypeStruct((path_rows, sims), jnp.float32),
        in_specs=[smem, smem, vmem, vmem, hbm, hbm],
        out_specs=vmem,
        scratch_shapes=[
            pltpu.VMEM((blocks, capacity, rank_cap), jnp.bfloat16),
            pltpu.VMEM((blocks, rank_cap, sims), jnp.bfloat16),
            pltpu.VMEM((padded, sims), jnp.float32),
            pltpu.VMEM((padded, sims), jnp.float32),
            pltpu.VMEM((padded, sims), jnp.float32),
            pltpu.VMEM((8, 128), jnp.float32),
            pltpu.VMEM((8, 128), jnp.float32),
            pltpu.VMEM((padded, sims), jnp.bfloat16),
            pltpu.VMEM((n * rows, sims), jnp.bfloat16),
            pltpu.VMEM((path_rows, n * rows), jnp.bfloat16),
            pltpu.VMEM((path_rows, 1), jnp.float32),
            dma((blocks,)), dma((blocks,)), dma, dma, dma, dma,
            dma((quads,)), dma((quads,)), dma((quads, QUAD)), dma((quads, QUAD)),
        ],
        compiler_params=pltpu.CompilerParams(
            collective_id=0, has_side_effects=True, vmem_limit_bytes=50 * 1024 * 1024
        ),
        name="gene_sets",
    )(block_len, block_rank, gene_span.T, gene_pathways.T, factor, normals)


def solution(mesh):
    in_specs = (
        P(("groups", "genome"), None, None),
        P(("groups", "genome"), None, None),
        P(("groups", "genome")),
        P(("groups", "genome")),
        P(("groups", "genome"), None),
        P("groups", None),
    )
    out_specs = P(("groups", "genome"), None)
    return jax.shard_map(local, mesh=mesh, in_specs=in_specs, out_specs=out_specs, check_vma=False)
```

time: 141 us -> 30.7 us (0.22)
  starting transfers between devices: 80 us -> 0 us
  matrix products: 31.9 us -> 0 us
  Pallas kernels: 0 us -> 25.4 us
  waiting for transfers between devices: 11.3 us -> 0 us
  other arithmetic: 10.6 us -> 0 us
    all_to_all x1 -> x0, starting transfers between devices: 78.5 us -> none  [local(): lax.all_to_all(packed, 'genome', split_axis=0, concat_axis=0, tiled=True)]
    dot_general x8 -> x0, matrix products: 31.9 us -> none  [the longest x3 15.1 us: local(): jnp.dot(covered(positions, gene_span), squares, precision=lax.Precision.H...]
    pallas_call x0 -> x1, Pallas kernels: none -> 25.4 us  [local(): pl.pallas_call(functools.partial(kernel, n, genes, rows), out_shape=jax.S...]
    all_to_all x1 -> x0, waiting for transfers between devices: 11.3 us -> none  [local(): lax.all_to_all(packed, 'genome', split_axis=0, concat_axis=0, tiled=True)]
    select_n x7 -> x0, other arithmetic: 7.35 us -> none  [the longest x1 4.67 us: local(): squares = jnp.where(usable[:, None], coloured * coloured, 0.0)]
    unnamed x11, local copies, waits for them, and re-layouts: 1.28 us -> 5.08 us
    gather x2 -> x0, local copies, waits for them, and re-layouts: 2.9 us -> none  [the longest x1 1.72 us: local(): local_path = gene_pathways.reshape(-1)[global_pair] - device * path_rows]
    lt x5 -> x0, other arithmetic: 2.59 us -> none  [the longest x3 1.79 us: local(): usable = row_ids < block_len[block]]
  transfers between devices with their start and end apart: 2 -> 0, of which waited for: 1 -> 0; matrix products, arithmetic and copies ran while one was open for 18% -> 0% of each run, Pallas kernels for 0% -> 0%
where the time goes in v1:
time: 30.7 us; the launch traced here: 30.5 us
  Pallas kernels  25.4 us (83%)
  local copies, waits for them, and re-layouts  5.08 us (17%)
    pallas_call x1, Pallas kernels, local(): pl.pallas_call(functools.partial(kernel, n, genes, rows), out_shape=jax.S...  25.4 us
    unnamed x11, local copies, waits for them, and re-layouts  5.08 us

profile of v1, /device:TPU:0, one launch (start us, length us, event | category | flops | bytes accessed | tf_op | source)
XLA Modules:
  0.0 30.5 jit_solution(5907033493083015910)
XLA Ops:
  0.0 0.0 copy-start
  0.0 1.4 %copy-done = bf16[3,256,1024]{2,1,0:T(8,128)(2,1)S(1)} copy-done((bf16[3,256,1024]{2,1,0:T(8,128)(2,1)S(1)}, bf16[3,256,1024]{2,1,0:T(8,128)(2,1)}, u32[]{:S(2)}) %copy-start) | copy-done | bytes 1572888
  1.4 0.0 copy-start.1
  1.4 0.7 %copy-done.1 = s32[1024,4]{0,1:T(4,128)S(1)} copy-done((s32[1024,4]{0,1:T(4,128)S(1)}, s32[1024,4]{0,1:T(4,128)}, u32[]{:S(2)}) %copy-start.1) | copy-done | bytes 16408
  2.1 0.0 copy-start.2
  2.1 0.7 %copy-done.2 = s32[64,2]{0,1:T(2,128)S(1)} copy-done((s32[64,2]{0,1:T(2,128)S(1)}, s32[64,2]{0,1:T(2,128)}, u32[]{:S(2)}) %copy-start.2) | copy-done | bytes 536
  2.8 0.0 copy-start.3
  2.8 0.7 %copy-done.3 = s32[3]{0:T(128)S(1)} copy-done((s32[3]{0:T(128)S(1)}, s32[3]{0:T(128)}, u32[]{:S(2)}) %copy-start.3) | copy-done | bytes 36
  3.5 0.0 copy-start.4
  3.5 0.7 %copy-done.4 = s32[3]{0:T(128)S(1)} copy-done((s32[3]{0:T(128)S(1)}, s32[3]{0:T(128)}, u32[]{:S(2)}) %copy-start.4) | copy-done | bytes 36
  4.1 25.4 %gene_sets.1 = f32[256,1024]{1,0:T(8,128)S(1)} custom-call(s32[3]{0:T(128)S(1)} %copy-done.3, s32[3]{0:T(128)S(1)} %copy-done.4, s32[2,64]{1,0:T(2,128)S(1)} %bitcast.3, s32[4,1024]{1,0:T(4,128)S(1)} %bitcast.2, bf16[3,2048,256]{2,1,0:T(8,128)(2,1)} %factor_ref.1, bf16[3,256,1024]{2,1,0:T(8,128)(2,1)S(1)} %copy-done), custom_call_target="tpu_custom_call" | custom-call | tf_op jit(solution)/shard_map/gene_sets/pallas_call | solution.py:200
  29.5 1.0 %copy.8 = f32[256,1024]{1,0:T(8,128)} copy(f32[256,1024]{1,0:T(8,128)S(1)} %gene_sets.1) | data formatting | bytes 2097152
Async XLA Ops:
  0.0 1.4 %copy-start = (bf16[3,256,1024]{2,1,0:T(8,128)(2,1)S(1)}, bf16[3,256,1024]{2,1,0:T(8,128)(2,1)}, u32[]{:S(2)}) copy-start(bf16[3,256,1024]{2,1,0:T(8,128)(2,1)} %normals_ref.1) | copy-start | bytes 4718596
  1.4 0.7 %copy-start.1 = (s32[1024,4]{0,1:T(4,128)S(1)}, s32[1024,4]{0,1:T(4,128)}, u32[]{:S(2)}) copy-start(s32[1024,4]{0,1:T(4,128)} %param.11) | copy-start | bytes 49156
  2.1 0.7 %copy-start.2 = (s32[64,2]{0,1:T(2,128)S(1)}, s32[64,2]{0,1:T(2,128)}, u32[]{:S(2)}) copy-start(s32[64,2]{0,1:T(2,128)} %param.10) | copy-start | bytes 1540
  2.8 0.7 %copy-start.3 = (s32[3]{0:T(128)S(1)}, s32[3]{0:T(128)}, u32[]{:S(2)}) copy-start(s32[3]{0:T(128)} %len_ref.1) | copy-start | bytes 40
  3.5 0.7 %copy-start.4 = (s32[3]{0:T(128)S(1)}, s32[3]{0:T(128)}, u32[]{:S(2)}) copy-start(s32[3]{0:T(128)} %rank_ref.1) | copy-start | bytes 40

commit v2 on v1

v2 whole, which is shorter than its diff:
```python
import functools

import jax
import jax.numpy as jnp
from jax import lax
from jax.experimental import pallas as pl
from jax.experimental.pallas import tpu as pltpu
from jax.sharding import PartitionSpec as P

PATHWAYS = 4096
PIECE = 256
TILE = 1024
QUAD = 4


def kernel(
    n, genes, rows,
    len_hbm, rank_hbm, span_hbm, paths_hbm, factor_ref, normals_ref,
    out_ref,
    len_ref, rank_ref, span_ref, paths_ref, fac, nrm, cover, cover_both,
    sums, partial, halo, own_span, pred_span, stat, gathered, member, count, result,
    small_sem, fac_sem, nrm_sem, span_send, span_recv, halo_send, halo_recv,
    col_send, col_recv, quad_send, quad_recv, out_sem,
):
    quads = n // QUAD
    blocks, capacity, rank_cap = factor_ref.shape
    sims = normals_ref.shape[2]
    pieces = sims // PIECE
    local_vars = blocks * capacity
    padded = quads * rows
    path_rows, total_genes = out_ref.shape[0], paths_ref.shape[1]
    slots = n * rows
    me = lax.axis_index("genome")
    right, left = lax.rem(me + 1, n), lax.rem(me + n - 1, n)
    quad, lane = me // QUAD, lax.rem(me, QUAD)
    column = [lax.rem(quad + d, quads) * QUAD + lane for d in range(1, quads)]
    peers = [quad * QUAD + lax.rem(lane + e, QUAD) for e in range(1, QUAD)]

    barrier = pltpu.get_barrier_semaphore()
    greeted = [left, right] + column + peers
    for device in greeted:
        pl.semaphore_signal(barrier, inc=1, device_id={"genome": device})

    small = [
        pltpu.make_async_copy(source, target, small_sem.at[i])
        for i, (source, target) in enumerate(
            [(span_hbm, span_ref), (rank_hbm, rank_ref), (len_hbm, len_ref), (paths_hbm, paths_ref)]
        )
    ]
    for copy in small:
        copy.start()
    order = list(range(1, blocks)) + [0]
    fac_copies, nrm_copies = {}, {}
    for b in order:
        nrm_copies[b] = pltpu.make_async_copy(normals_ref.at[b], nrm.at[b], nrm_sem.at[b])
        fac_copies[b] = pltpu.make_async_copy(factor_ref.at[b], fac.at[b], fac_sem.at[b])
        nrm_copies[b].start()
        fac_copies[b].start()

    share = genes // quads
    row = lax.broadcasted_iota(jnp.int32, (padded, genes), 0)
    col = lax.broadcasted_iota(jnp.int32, (padded, genes), 1)
    within = lax.rem(row, rows)
    placed = (lax.div(row, rows) + quads * within == col) & (within < share)

    def columns_of(spans):
        lower = jnp.sum(jnp.where(placed, spans[0:1, :genes], 0.0), axis=1, keepdims=True)
        upper = jnp.sum(jnp.where(placed, spans[1:2, :genes], 0.0), axis=1, keepdims=True)
        return lower.astype(jnp.int32), upper.astype(jnp.int32)

    slot = lax.broadcasted_iota(jnp.int32, (1, slots), 1)
    first_gene = lax.div(slot, rows) * genes + lax.rem(slot, rows) * quads
    first_gene = jnp.where(lax.rem(slot, rows) < share, first_gene, total_genes)
    gene = lax.broadcasted_iota(jnp.int32, (total_genes, slots), 0)
    takes = (gene >= first_gene) & (gene < first_gene + quads)
    takes = takes.astype(jnp.float32).astype(jnp.bfloat16)
    own_span[...] = jnp.zeros_like(own_span)
    for copy in small:
        copy.wait()
    own_span[0:2, 0:genes] = span_ref[...].astype(jnp.float32)
    lower, upper = columns_of(own_span[...])
    named = paths_ref[pl.ds(lane, 1), :] - me * path_rows
    ids = lax.broadcasted_iota(jnp.int32, (path_rows, total_genes), 0)
    names = (named == ids).astype(jnp.float32).astype(jnp.bfloat16)
    chosen = jnp.dot(names, takes, preferred_element_type=jnp.float32)
    count[...] = jnp.sum(chosen, axis=1, keepdims=True)
    member[...] = chosen.astype(jnp.bfloat16)

    def trim(b):
        nrm_copies[b].wait()
        kept = lax.broadcasted_iota(jnp.int32, (rank_cap, sims), 0) < rank_ref[b]
        nrm[b] = jnp.where(kept, nrm[b].astype(jnp.float32), 0.0).astype(jnp.bfloat16)

    def coverage(b, low, high):
        start = me * local_vars + b * capacity
        place = start + lax.broadcasted_iota(jnp.int32, (padded, capacity), 1)
        inside = (place >= low) & (place < jnp.minimum(high, start + len_ref[b]))
        return inside.astype(jnp.float32).astype(jnp.bfloat16)

    def coloured(b, piece, first):
        return jnp.dot(
            fac[b, pl.ds(first, TILE), :],
            nrm[b, :, pl.ds(piece * PIECE, PIECE)],
            preferred_element_type=jnp.float32,
        )

    def add_blocks(chain, piece):
        steps = [(b, first) for b in chain for first in range(0, capacity, TILE)]
        totals = {}
        ahead = coloured(steps[0][0], piece, steps[0][1])
        for at, (b, first) in enumerate(steps):
            squares = (ahead * ahead).astype(jnp.bfloat16)
            if at + 1 < len(steps):
                ahead = coloured(steps[at + 1][0], piece, steps[at + 1][1])
            rows_of = cover_both if b == 0 else cover.at[b]
            term = jnp.dot(
                rows_of[:, pl.ds(first, TILE)], squares, preferred_element_type=jnp.float32
            )
            totals[b] = totals[b] + term if b in totals else term
        kept = None
        for b, total in totals.items():
            if b == 0:
                partial[piece] = total[padded:]
                total = total[:padded]
            kept = total if kept is None else kept + total
        return kept

    halo_copies = [
        pltpu.make_async_remote_copy(
            partial.at[piece], halo.at[piece], halo_send.at[piece], halo_recv.at[piece],
            device_id={"genome": left},
        )
        for piece in range(pieces)
    ]

    def send_halo(piece):
        @pl.when(me > 0)
        def _():
            halo_copies[piece].start()

    scale = 1.0 / capacity
    col_copies, quad_copies = {}, {}

    def slot_rows(index):
        return pl.ds(pl.multiple_of(index * rows, rows), rows)

    def forward(piece, d):
        source = lax.rem(quad + quads - d, quads) * QUAD + lane
        block = gathered.at[piece, slot_rows(source)]
        for e in range(1, QUAD):
            copy = pltpu.make_async_remote_copy(
                block, block, quad_send.at[piece, d, e], quad_recv.at[piece, d, e],
                device_id={"genome": peers[e - 1]},
            )
            copy.start()
            quad_copies[piece, d, e] = copy

    def finish_stat(piece):
        @pl.when(me < n - 1)
        def _():
            halo_copies[piece].wait_recv()
            stat[piece] = ((sums[piece] + halo[piece]) * scale).astype(jnp.bfloat16)

        @pl.when(me == n - 1)
        def _():
            stat[piece] = (sums[piece] * scale).astype(jnp.bfloat16)

        for d in range(1, quads):
            target = lax.rem(quad + d, quads)
            copy = pltpu.make_async_remote_copy(
                stat.at[piece, slot_rows(target)], gathered.at[piece, slot_rows(me)],
                col_send.at[piece, d], col_recv.at[piece, d],
                device_id={"genome": target * QUAD + lane},
            )
            copy.start()
            col_copies[piece, d] = copy
        gathered[piece, slot_rows(me), :] = stat[piece, slot_rows(quad), :]
        forward(piece, 0)

    def pass_on(piece):
        for d in range(1, quads):
            col_copies[piece, d].wait_recv()
            forward(piece, d)

    out_copies = []

    def score(piece):
        for d in range(quads):
            for e in range(1, QUAD):
                quad_copies[piece, d, e].wait_recv()
        summed = jnp.dot(member[...], gathered[piece], preferred_element_type=jnp.float32)
        result[piece] = summed / count[...]
        copy = pltpu.make_async_copy(
            result.at[piece], out_ref.at[:, pl.ds(piece * PIECE, PIECE)], out_sem.at[piece]
        )
        copy.start()
        out_copies.append(copy)

    for piece in range(pieces):
        if piece == 0:
            span_copy = pltpu.make_async_remote_copy(
                own_span, pred_span, span_send, span_recv, device_id={"genome": right}
            )
            total = None
            for b in order:
                trim(b)
                fac_copies[b].wait()
                if b == 0:
                    span_copy.wait()
                    cover_both[:padded] = coverage(0, lower, upper)
                    cover_both[padded:] = coverage(0, *columns_of(pred_span[...]))
                else:
                    cover[b] = coverage(b, lower, upper)
                term = add_blocks([b], piece)
                total = term if total is None else total + term
                if b == order[0]:
                    pl.semaphore_wait(barrier, len(greeted))
                    span_copy.start()
            sums[piece] = total
            send_halo(piece)
        else:
            total = add_blocks([0], piece)
            send_halo(piece)
            finish_stat(piece - 1)
            if piece > 1:
                score(piece - 2)
            sums[piece] = total + add_blocks(order[:-1], piece)
            pass_on(piece - 1)
    finish_stat(pieces - 1)
    score(pieces - 2)
    pass_on(pieces - 1)
    score(pieces - 1)

    for piece in range(pieces):
        @pl.when(me > 0)
        def _():
            halo_copies[piece].wait_send()
    for copy in list(col_copies.values()) + list(quad_copies.values()):
        copy.wait_send()
    for copy in out_copies:
        copy.wait()


def local(factor, normals, block_len, block_rank, gene_span, gene_pathways):
    blocks, capacity, rank_cap = factor.shape
    sims = normals.shape[2]
    genes = gene_span.shape[0]
    total_genes, members = gene_pathways.shape
    n = lax.axis_size("genome")
    quads = n // QUAD
    rows = max(16, genes // quads)
    padded = quads * rows
    pieces = sims // PIECE
    path_rows = PATHWAYS // n
    hbm = pl.BlockSpec(memory_space=pltpu.HBM)
    dma = pltpu.SemaphoreType.DMA
    return pl.pallas_call(
        functools.partial(kernel, n, genes, rows),
        out_shape=jax.ShapeDtypeStruct((path_rows, sims), jnp.float32),
        in_specs=[hbm] * 6,
        out_specs=hbm,
        scratch_shapes=[
            pltpu.SMEM((blocks,), jnp.int32),
            pltpu.SMEM((blocks,), jnp.int32),
            pltpu.VMEM((2, genes), jnp.int32),
            pltpu.VMEM((members, total_genes), jnp.int32),
            pltpu.VMEM((blocks, capacity, rank_cap), jnp.bfloat16),
            pltpu.VMEM((blocks, rank_cap, sims), jnp.bfloat16),
            pltpu.VMEM((blocks, padded, capacity), jnp.bfloat16),
            pltpu.VMEM((2 * padded, capacity), jnp.bfloat16),
            pltpu.VMEM((pieces, padded, PIECE), jnp.float32),
            pltpu.VMEM((pieces, padded, PIECE), jnp.float32),
            pltpu.VMEM((pieces, padded, PIECE), jnp.float32),
            pltpu.VMEM((8, 128), jnp.float32),
            pltpu.VMEM((8, 128), jnp.float32),
            pltpu.VMEM((pieces, padded, PIECE), jnp.bfloat16),
            pltpu.VMEM((pieces, n * rows, PIECE), jnp.bfloat16),
            pltpu.VMEM((path_rows, n * rows), jnp.bfloat16),
            pltpu.VMEM((path_rows, 1), jnp.float32),
            pltpu.VMEM((pieces, path_rows, PIECE), jnp.float32),
            dma((4,)), dma((blocks,)), dma((blocks,)), dma, dma, dma((pieces,)), dma((pieces,)),
            dma((pieces, quads)), dma((pieces, quads)),
            dma((pieces, quads, QUAD)), dma((pieces, quads, QUAD)), dma((pieces,)),
        ],
        compiler_params=pltpu.CompilerParams(
            collective_id=0, has_side_effects=True, vmem_limit_bytes=56 * 1024 * 1024
        ),
        name="gene_sets",
    )(block_len, block_rank, gene_span.T, gene_pathways.T, factor, normals)


def solution(mesh):
    in_specs = (
        P(("groups", "genome"), None, None),
        P(("groups", "genome"), None, None),
        P(("groups", "genome")),
        P(("groups", "genome")),
        P(("groups", "genome"), None),
        P("groups", None),
    )
    out_specs = P(("groups", "genome"), None)
    return jax.shard_map(local, mesh=mesh, in_specs=in_specs, out_specs=out_specs, check_vma=False)
```

time: 30.7 us -> 35.9 us (1.17)
  Pallas kernels: 25.4 us -> 33.4 us
  local copies, waits for them, and re-layouts: 5.08 us -> 2.31 us
    pallas_call x1, Pallas kernels: 25.4 us -> 33.4 us  [local(): pl.pallas_call(functools.partial(kernel, n, genes, rows), out_shape=jax.S...]
    unnamed x11 -> x1, local copies, waits for them, and re-layouts: 5.08 us -> 2.31 us
where the time goes in v2:
time: 35.9 us; the launch traced here: 35.7 us
  Pallas kernels  33.4 us (93%)
  local copies, waits for them, and re-layouts  2.31 us (6%)
    pallas_call x1, Pallas kernels, local(): pl.pallas_call(functools.partial(kernel, n, genes, rows), out_shape=jax.S...  33.4 us
    unnamed x1, local copies, waits for them, and re-layouts  2.31 us

profile of v2, /device:TPU:0, one launch (start us, length us, event | category | flops | bytes accessed | tf_op | source)
XLA Modules:
  0.0 35.7 jit_solution(7469959651069764987)
XLA Ops:
  0.0 33.4 %gene_sets.1 = f32[256,1024]{1,0:T(8,128)} custom-call(s32[3]{0:T(128)} %len_hbm.1, s32[3]{0:T(128)} %rank_hbm.1, s32[2,64]{1,0:T(2,128)} %bitcast.3, s32[4,1024]{1,0:T(4,128)} %bitcast.2, bf16[3,2048,256]{2,1,0:T(8,128)(2,1)} %factor_ref.1, bf16[3,256,1024]{2,1,0:T(8,128)(2,1)} %normals_ref.1), custom_call_target="tpu_custom_call" | custom-call | tf_op jit(solution)/shard_map/gene_sets/pallas_call | solution.py:257
  33.4 2.3 %copy.8 = f32[256,1024]{1,0:T(8,128)} copy(f32[256,1024]{1,0:T(8,128)} %gene_sets.1) | data formatting | bytes 2097152

commit v3 on v2

--- a/solution.py
+++ b/solution.py
@@ -8,8 +8,8 @@
 from jax.sharding import PartitionSpec as P
 
 PATHWAYS = 4096
-PIECE = 256
-TILE = 1024
+PIECE = 512
+TILE = 512
 QUAD = 4
 
 
@@ -18,9 +18,9 @@
     len_hbm, rank_hbm, span_hbm, paths_hbm, factor_ref, normals_ref,
     out_ref,
     len_ref, rank_ref, span_ref, paths_ref, fac, nrm, cover, cover_both,
-    sums, partial, halo, own_span, pred_span, stat, gathered, member, count, result,
+    sums, partial, halo, own_span, pred_span, stat, gathered, member, count,
     small_sem, fac_sem, nrm_sem, span_send, span_recv, halo_send, halo_recv,
-    col_send, col_recv, quad_send, quad_recv, out_sem,
+    col_send, col_recv, quad_send, quad_recv,
 ):
     quads = n // QUAD
     blocks, capacity, rank_cap = factor_ref.shape
@@ -107,11 +107,9 @@
     def add_blocks(chain, piece):
         steps = [(b, first) for b in chain for first in range(0, capacity, TILE)]
         totals = {}
-        ahead = coloured(steps[0][0], piece, steps[0][1])
-        for at, (b, first) in enumerate(steps):
-            squares = (ahead * ahead).astype(jnp.bfloat16)
-            if at + 1 < len(steps):
-                ahead = coloured(steps[at + 1][0], piece, steps[at + 1][1])
+        for b, first in steps:
+            values = coloured(b, piece, first)
+            squares = (values * values).astype(jnp.bfloat16)
             rows_of = cover_both if b == 0 else cover.at[b]
             term = jnp.dot(
                 rows_of[:, pl.ds(first, TILE)], squares, preferred_element_type=jnp.float32
@@ -182,19 +180,12 @@
             col_copies[piece, d].wait_recv()
             forward(piece, d)
 
-    out_copies = []
-
     def score(piece):
         for d in range(quads):
             for e in range(1, QUAD):
                 quad_copies[piece, d, e].wait_recv()
         summed = jnp.dot(member[...], gathered[piece], preferred_element_type=jnp.float32)
-        result[piece] = summed / count[...]
-        copy = pltpu.make_async_copy(
-            result.at[piece], out_ref.at[:, pl.ds(piece * PIECE, PIECE)], out_sem.at[piece]
-        )
-        copy.start()
-        out_copies.append(copy)
+        out_ref[:, pl.ds(piece * PIECE, PIECE)] = summed / count[...]
 
     for piece in range(pieces):
         if piece == 0:
@@ -237,8 +228,6 @@
             halo_copies[piece].wait_send()
     for copy in list(col_copies.values()) + list(quad_copies.values()):
         copy.wait_send()
-    for copy in out_copies:
-        copy.wait()
 
 
 def local(factor, normals, block_len, block_rank, gene_span, gene_pathways):
@@ -258,7 +247,7 @@
         functools.partial(kernel, n, genes, rows),
         out_shape=jax.ShapeDtypeStruct((path_rows, sims), jnp.float32),
         in_specs=[hbm] * 6,
-        out_specs=hbm,
+        out_specs=pl.BlockSpec(memory_space=pltpu.VMEM),
         scratch_shapes=[
             pltpu.SMEM((blocks,), jnp.int32),
             pltpu.SMEM((blocks,), jnp.int32),
@@ -277,13 +266,12 @@
             pltpu.VMEM((pieces, n * rows, PIECE), jnp.bfloat16),
             pltpu.VMEM((path_rows, n * rows), jnp.bfloat16),
             pltpu.VMEM((path_rows, 1), jnp.float32),
-            pltpu.VMEM((pieces, path_rows, PIECE), jnp.float32),
             dma((4,)), dma((blocks,)), dma((blocks,)), dma, dma, dma((pieces,)), dma((pieces,)),
             dma((pieces, quads)), dma((pieces, quads)),
-            dma((pieces, quads, QUAD)), dma((pieces, quads, QUAD)), dma((pieces,)),
+            dma((pieces, quads, QUAD)), dma((pieces, quads, QUAD)),
         ],
         compiler_params=pltpu.CompilerParams(
-            collective_id=0, has_side_effects=True, vmem_limit_bytes=56 * 1024 * 1024
+            collective_id=0, has_side_effects=True, vmem_limit_bytes=50 * 1024 * 1024
         ),
         name="gene_sets",
     )(block_len, block_rank, gene_span.T, gene_pathways.T, factor, normals)

time: 35.9 us -> 31 us (0.86)
  Pallas kernels: 33.4 us -> 25.6 us
  local copies, waits for them, and re-layouts: 2.31 us -> 5.08 us
    pallas_call x1, Pallas kernels: 33.4 us -> 25.6 us  [local(): pl.pallas_call(functools.partial(kernel, n, genes, rows), out_shape=jax.S...]
    unnamed x1 -> x11, local copies, waits for them, and re-layouts: 2.31 us -> 5.08 us
where the time goes in v3:
time: 31 us; the launch traced here: 30.7 us
  Pallas kernels  25.6 us (83%)
  local copies, waits for them, and re-layouts  5.08 us (16%)
    pallas_call x1, Pallas kernels, local(): pl.pallas_call(functools.partial(kernel, n, genes, rows), out_shape=jax.S...  25.6 us
    unnamed x11, local copies, waits for them, and re-layouts  5.08 us

profile of v3, /device:TPU:0, one launch (start us, length us, event | category | flops | bytes accessed | tf_op | source)
XLA Modules:
  0.0 30.7 jit_solution(2566074344966060923)
XLA Ops:
  0.0 0.0 copy-start
  0.0 1.4 %copy-done = bf16[3,256,1024]{2,1,0:T(8,128)(2,1)S(1)} copy-done((bf16[3,256,1024]{2,1,0:T(8,128)(2,1)S(1)}, bf16[3,256,1024]{2,1,0:T(8,128)(2,1)}, u32[]{:S(2)}) %copy-start) | copy-done | bytes 1572888
  1.4 0.0 copy-start.1
  1.4 0.7 %copy-done.1 = s32[1024,4]{0,1:T(4,128)S(1)} copy-done((s32[1024,4]{0,1:T(4,128)S(1)}, s32[1024,4]{0,1:T(4,128)}, u32[]{:S(2)}) %copy-start.1) | copy-done | bytes 16408
  2.1 0.0 copy-start.2
  2.1 0.7 %copy-done.2 = s32[64,2]{0,1:T(2,128)S(1)} copy-done((s32[64,2]{0,1:T(2,128)S(1)}, s32[64,2]{0,1:T(2,128)}, u32[]{:S(2)}) %copy-start.2) | copy-done | bytes 536
  2.8 0.0 copy-start.3
  2.8 0.7 %copy-done.3 = s32[3]{0:T(128)S(1)} copy-done((s32[3]{0:T(128)S(1)}, s32[3]{0:T(128)}, u32[]{:S(2)}) %copy-start.3) | copy-done | bytes 36
  3.5 0.0 copy-start.4
  3.5 0.7 %copy-done.4 = s32[3]{0:T(128)S(1)} copy-done((s32[3]{0:T(128)S(1)}, s32[3]{0:T(128)}, u32[]{:S(2)}) %copy-start.4) | copy-done | bytes 36
  4.1 25.6 %gene_sets.1 = f32[256,1024]{1,0:T(8,128)S(1)} custom-call(s32[3]{0:T(128)S(1)} %copy-done.3, s32[3]{0:T(128)S(1)} %copy-done.4, s32[2,64]{1,0:T(2,128)S(1)} %bitcast.3, s32[4,1024]{1,0:T(4,128)S(1)} %bitcast.2, bf16[3,2048,256]{2,1,0:T(8,128)(2,1)} %factor_ref.1, bf16[3,256,1024]{2,1,0:T(8,128)(2,1)S(1)} %copy-done), custom_call_target="tpu_custom_call" | custom-call | tf_op jit(solution)/shard_map/gene_sets/pallas_call | solution.py:246
  29.7 1.0 %copy.8 = f32[256,1024]{1,0:T(8,128)} copy(f32[256,1024]{1,0:T(8,128)S(1)} %gene_sets.1) | data formatting | bytes 2097152
Async XLA Ops:
  0.0 1.4 %copy-start = (bf16[3,256,1024]{2,1,0:T(8,128)(2,1)S(1)}, bf16[3,256,1024]{2,1,0:T(8,128)(2,1)}, u32[]{:S(2)}) copy-start(bf16[3,256,1024]{2,1,0:T(8,128)(2,1)} %normals_ref.1) | copy-start | bytes 4718596
  1.4 0.7 %copy-start.1 = (s32[1024,4]{0,1:T(4,128)S(1)}, s32[1024,4]{0,1:T(4,128)}, u32[]{:S(2)}) copy-start(s32[1024,4]{0,1:T(4,128)} %param.11) | copy-start | bytes 49156
  2.1 0.7 %copy-start.2 = (s32[64,2]{0,1:T(2,128)S(1)}, s32[64,2]{0,1:T(2,128)}, u32[]{:S(2)}) copy-start(s32[64,2]{0,1:T(2,128)} %param.10) | copy-start | bytes 1540
  2.8 0.7 %copy-start.3 = (s32[3]{0:T(128)S(1)}, s32[3]{0:T(128)}, u32[]{:S(2)}) copy-start(s32[3]{0:T(128)} %len_hbm.1) | copy-start | bytes 40
  3.5 0.7 %copy-start.4 = (s32[3]{0:T(128)S(1)}, s32[3]{0:T(128)}, u32[]{:S(2)}) copy-start(s32[3]{0:T(128)} %rank_hbm.1) | copy-start | bytes 40

commit v4 on v2

--- a/solution.py
+++ b/solution.py
@@ -8,15 +8,15 @@
 from jax.sharding import PartitionSpec as P
 
 PATHWAYS = 4096
-PIECE = 256
-TILE = 1024
+PIECE = 512
+TILE = 2048
 QUAD = 4
 
 
 def kernel(
     n, genes, rows,
     len_hbm, rank_hbm, span_hbm, paths_hbm, factor_ref, normals_ref,
-    out_ref,
+    out_ref, count_hbm,
     len_ref, rank_ref, span_ref, paths_ref, fac, nrm, cover, cover_both,
     sums, partial, halo, own_span, pred_span, stat, gathered, member, count, result,
     small_sem, fac_sem, nrm_sem, span_send, span_recv, halo_send, halo_recv,
@@ -83,8 +83,11 @@
     ids = lax.broadcasted_iota(jnp.int32, (path_rows, total_genes), 0)
     names = (named == ids).astype(jnp.float32).astype(jnp.bfloat16)
     chosen = jnp.dot(names, takes, preferred_element_type=jnp.float32)
-    count[...] = jnp.sum(chosen, axis=1, keepdims=True)
+    count[...] = jnp.broadcast_to(jnp.sum(chosen, axis=1, keepdims=True), count.shape)
     member[...] = chosen.astype(jnp.bfloat16)
+
+    count_copy = pltpu.make_async_copy(count, count_hbm, out_sem.at[pieces])
+    count_copy.start()
 
     def trim(b):
         nrm_copies[b].wait()
@@ -107,11 +110,9 @@
     def add_blocks(chain, piece):
         steps = [(b, first) for b in chain for first in range(0, capacity, TILE)]
         totals = {}
-        ahead = coloured(steps[0][0], piece, steps[0][1])
-        for at, (b, first) in enumerate(steps):
-            squares = (ahead * ahead).astype(jnp.bfloat16)
-            if at + 1 < len(steps):
-                ahead = coloured(steps[at + 1][0], piece, steps[at + 1][1])
+        for b, first in steps:
+            values = coloured(b, piece, first)
+            squares = (values * values).astype(jnp.bfloat16)
             rows_of = cover_both if b == 0 else cover.at[b]
             term = jnp.dot(
                 rows_of[:, pl.ds(first, TILE)], squares, preferred_element_type=jnp.float32
@@ -182,14 +183,15 @@
             col_copies[piece, d].wait_recv()
             forward(piece, d)
 
-    out_copies = []
+    out_copies = [count_copy]
 
     def score(piece):
         for d in range(quads):
             for e in range(1, QUAD):
                 quad_copies[piece, d, e].wait_recv()
-        summed = jnp.dot(member[...], gathered[piece], preferred_element_type=jnp.float32)
-        result[piece] = summed / count[...]
+        result[piece] = jnp.dot(
+            member[...], gathered[piece], preferred_element_type=jnp.float32
+        )
         copy = pltpu.make_async_copy(
             result.at[piece], out_ref.at[:, pl.ds(piece * PIECE, PIECE)], out_sem.at[piece]
         )
@@ -254,11 +256,14 @@
     path_rows = PATHWAYS // n
     hbm = pl.BlockSpec(memory_space=pltpu.HBM)
     dma = pltpu.SemaphoreType.DMA
-    return pl.pallas_call(
+    summed, count = pl.pallas_call(
         functools.partial(kernel, n, genes, rows),
-        out_shape=jax.ShapeDtypeStruct((path_rows, sims), jnp.float32),
+        out_shape=[
+            jax.ShapeDtypeStruct((path_rows, sims), jnp.float32),
+            jax.ShapeDtypeStruct((path_rows, 128), jnp.float32),
+        ],
         in_specs=[hbm] * 6,
-        out_specs=hbm,
+        out_specs=[hbm, hbm],
         scratch_shapes=[
             pltpu.SMEM((blocks,), jnp.int32),
             pltpu.SMEM((blocks,), jnp.int32),
@@ -276,17 +281,18 @@
             pltpu.VMEM((pieces, padded, PIECE), jnp.bfloat16),
             pltpu.VMEM((pieces, n * rows, PIECE), jnp.bfloat16),
             pltpu.VMEM((path_rows, n * rows), jnp.bfloat16),
-            pltpu.VMEM((path_rows, 1), jnp.float32),
+            pltpu.VMEM((path_rows, 128), jnp.float32),
             pltpu.VMEM((pieces, path_rows, PIECE), jnp.float32),
             dma((4,)), dma((blocks,)), dma((blocks,)), dma, dma, dma((pieces,)), dma((pieces,)),
             dma((pieces, quads)), dma((pieces, quads)),
-            dma((pieces, quads, QUAD)), dma((pieces, quads, QUAD)), dma((pieces,)),
+            dma((pieces, quads, QUAD)), dma((pieces, quads, QUAD)), dma((pieces + 1,)),
         ],
         compiler_params=pltpu.CompilerParams(
-            collective_id=0, has_side_effects=True, vmem_limit_bytes=56 * 1024 * 1024
+            collective_id=0, has_side_effects=True, vmem_limit_bytes=60 * 1024 * 1024
         ),
         name="gene_sets",
     )(block_len, block_rank, gene_span.T, gene_pathways.T, factor, normals)
+    return summed / jnp.concatenate([count] * (sims // 128), axis=1)
 
 
 def solution(mesh):

time: 35.9 us -> 36.9 us (1.028)
  Pallas kernels: 33.4 us -> 26.9 us
  local copies, waits for them, and re-layouts: 2.31 us -> 7.34 us
  other arithmetic: 0 us -> 2.4 us
    pallas_call x1, Pallas kernels: 33.4 us -> 26.9 us  [local(): pl.pallas_call(functools.partial(kernel, n, genes, rows), out_shape=[jax....]
    unnamed x1 -> x7, local copies, waits for them, and re-layouts: 2.31 us -> 6.42 us
    div x0 -> x1, other arithmetic: none -> 2.4 us  [local(): return summed / jnp.concatenate([count] * (sims // 128), axis=1)]
    concatenate x0 -> x1, local copies, waits for them, and re-layouts: none -> 0.92 us  [local(): return summed / jnp.concatenate([count] * (sims // 128), axis=1)]
where the time goes in v4:
time: 36.9 us; the launch traced here: 36.6 us
  Pallas kernels  26.9 us (73%)
  local copies, waits for them, and re-layouts  7.34 us (20%)
  other arithmetic  2.4 us (7%)
    pallas_call x1, Pallas kernels, local(): pl.pallas_call(functools.partial(kernel, n, genes, rows), out_shape=[jax....  26.9 us
    unnamed x7, local copies, waits for them, and re-layouts  6.42 us
    div x1, other arithmetic, local(): return summed / jnp.concatenate([count] * (sims // 128), axis=1)  2.4 us
    concatenate x1, local copies, waits for them, and re-layouts, local(): return summed / jnp.concatenate([count] * (sims // 128), axis=1)  0.92 us

profile of v4, /device:TPU:0, one launch (start us, length us, event | category | flops | bytes accessed | tf_op | source)
XLA Modules:
  0.0 36.6 jit_solution(9133691932286147702)
XLA Ops:
  0.0 26.9 %gene_sets.1 = (f32[256,1024]{1,0:T(8,128)}, f32[256,128]{1,0:T(8,128)}) custom-call(s32[3]{0:T(128)} %len_hbm.1, s32[3]{0:T(128)} %rank_hbm.1, s32[2,64]{1,0:T(2,128)} %bitcast.3, s32[4,1024]{1,0:T(4,128)} %bitcast.2, bf16[3,2048,256]{2,1,0:T(8,128)(2,1)} %factor_ref.1, bf16[3,256,1024]{2,1,0:T(8,128)(2,1)} %normals_ref.1), custom_call_target="tpu_custom_call" | custom-call | tf_op jit(solution)/shard_map/gene_sets/pallas_call | solution.py:259
  26.9 0.9 %constant_dynamic-update-slice_fusion.7 = f32[256,1024]{1,0:T(8,128)S(1)} fusion(f32[256,128]{1,0:T(8,128)} %get-tuple-element.8), kind=kLoop, calls=%fused_computation.7 | loop fusion | bytes 262144
  27.8 0.9 %constant_dynamic-update-slice_fusion.6 = f32[256,1024]{1,0:T(8,128)S(1)} fusion(f32[256,1024]{1,0:T(8,128)S(1)} %constant_dynamic-update-slice_fusion.7, f32[256,128]{1,0:T(8,128)} %get-tuple-element.8), kind=kLoop, calls=%fused_computation.6 | loop fusion | bytes 262144
  28.7 0.9 %constant_dynamic-update-slice_fusion.5 = f32[256,1024]{1,0:T(8,128)S(1)} fusion(f32[256,1024]{1,0:T(8,128)S(1)} %constant_dynamic-update-slice_fusion.6, f32[256,128]{1,0:T(8,128)} %get-tuple-element.8), kind=kLoop, calls=%fused_computation.5 | loop fusion | bytes 262144
  29.6 0.9 %constant_dynamic-update-slice_fusion.4 = f32[256,1024]{1,0:T(8,128)S(1)} fusion(f32[256,1024]{1,0:T(8,128)S(1)} %constant_dynamic-update-slice_fusion.5, f32[256,128]{1,0:T(8,128)} %get-tuple-element.8), kind=kLoop, calls=%fused_computation.4 | loop fusion | bytes 262144
  30.5 0.9 %constant_dynamic-update-slice_fusion.3 = f32[256,1024]{1,0:T(8,128)S(1)} fusion(f32[256,1024]{1,0:T(8,128)S(1)} %constant_dynamic-update-slice_fusion.4, f32[256,128]{1,0:T(8,128)} %get-tuple-element.8), kind=kLoop, calls=%fused_computation.3 | loop fusion | bytes 262144
  31.5 0.9 %constant_dynamic-update-slice_fusion.2 = f32[256,1024]{1,0:T(8,128)S(1)} fusion(f32[256,1024]{1,0:T(8,128)S(1)} %constant_dynamic-update-slice_fusion.3, f32[256,128]{1,0:T(8,128)} %get-tuple-element.8), kind=kLoop, calls=%fused_computation.2 | loop fusion | bytes 262144
  32.4 0.9 %constant_dynamic-update-slice_fusion.1 = f32[256,1024]{1,0:T(8,128)S(1)} fusion(f32[256,1024]{1,0:T(8,128)S(1)} %constant_dynamic-update-slice_fusion.2, f32[256,128]{1,0:T(8,128)} %get-tuple-element.8), kind=kLoop, calls=%fused_computation.1 | loop fusion | bytes 262144
  33.3 0.9 %constant_dynamic-update-slice_fusion = f32[256,1024]{1,0:T(8,128)S(1)} fusion(f32[256,1024]{1,0:T(8,128)S(1)} %constant_dynamic-update-slice_fusion.1, f32[256,128]{1,0:T(8,128)} %get-tuple-element.8), kind=kLoop, calls=%fused_computation | loop fusion | bytes 262144 | tf_op jit(solution)/shard_map/concatenate | solution.py:295
  34.2 2.4 %div.3 = f32[256,1024]{1,0:T(8,128)} divide(f32[256,1024]{1,0:T(8,128)} %get-tuple-element.7, f32[256,1024]{1,0:T(8,128)S(1)} %constant_dynamic-update-slice_fusion) | non-fusion elementwise | flops 262144 | bytes 3145728 | tf_op jit(solution)/shard_map/div | solution.py:295

commit v5 on v3

--- a/solution.py
+++ b/solution.py
@@ -9,7 +9,7 @@
 
 PATHWAYS = 4096
 PIECE = 512
-TILE = 512
+TILE = 2048
 QUAD = 4
 
 
@@ -215,11 +215,14 @@
             finish_stat(piece - 1)
             if piece > 1:
                 score(piece - 2)
-            sums[piece] = total + add_blocks(order[:-1], piece)
-            pass_on(piece - 1)
+            for b in order[:-1]:
+                total += add_blocks([b], piece)
+                if b == order[0]:
+                    pass_on(piece - 1)
+            sums[piece] = total
     finish_stat(pieces - 1)
+    pass_on(pieces - 1)
     score(pieces - 2)
-    pass_on(pieces - 1)
     score(pieces - 1)
 
     for piece in range(pieces):
@@ -271,7 +274,7 @@
             dma((pieces, quads, QUAD)), dma((pieces, quads, QUAD)),
         ],
         compiler_params=pltpu.CompilerParams(
-            collective_id=0, has_side_effects=True, vmem_limit_bytes=50 * 1024 * 1024
+            collective_id=0, has_side_effects=True, vmem_limit_bytes=60 * 1024 * 1024
         ),
         name="gene_sets",
     )(block_len, block_rank, gene_span.T, gene_pathways.T, factor, normals)

time: 31 us -> 27.7 us (0.89)
  local copies, waits for them, and re-layouts: 5.08 us -> 2.31 us
  Pallas kernels: 25.6 us -> 25.2 us
    unnamed x11 -> x1, local copies, waits for them, and re-layouts: 5.08 us -> 2.31 us
    pallas_call x1, Pallas kernels: 25.6 us -> 25.2 us  [local(): pl.pallas_call(functools.partial(kernel, n, genes, rows), out_shape=jax.S...]
where the time goes in v5:
time: 27.7 us; the launch traced here: 27.5 us
  Pallas kernels  25.2 us (91%)
  local copies, waits for them, and re-layouts  2.31 us (8%)
    pallas_call x1, Pallas kernels, local(): pl.pallas_call(functools.partial(kernel, n, genes, rows), out_shape=jax.S...  25.2 us
    unnamed x1, local copies, waits for them, and re-layouts  2.31 us

profile of v5, /device:TPU:0, one launch (start us, length us, event | category | flops | bytes accessed | tf_op | source)
XLA Modules:
  0.0 27.5 jit_solution(18375221174774919109)
XLA Ops:
  0.0 25.2 %gene_sets.1 = f32[256,1024]{1,0:T(8,128)} custom-call(s32[3]{0:T(128)} %len_hbm.1, s32[3]{0:T(128)} %rank_hbm.1, s32[2,64]{1,0:T(2,128)} %bitcast.3, s32[4,1024]{1,0:T(4,128)} %bitcast.2, bf16[3,2048,256]{2,1,0:T(8,128)(2,1)} %factor_ref.1, bf16[3,256,1024]{2,1,0:T(8,128)(2,1)} %normals_ref.1), custom_call_target="tpu_custom_call" | custom-call | tf_op jit(solution)/shard_map/gene_sets/pallas_call | solution.py:249
  25.2 2.3 %copy.8 = f32[256,1024]{1,0:T(8,128)} copy(f32[256,1024]{1,0:T(8,128)} %gene_sets.1) | data formatting | bytes 2097152
